TPU v7x, 512 devices: a whole 4x4x16 slice. The times are simulated.
512 devices in a mesh: row: 16 (over y_hi, x, core), col: 16 (over z), vir: 2 (over y_lo).
Axes of the slice: x: 4, y: 4 (y_hi: 2, y_lo: 2; y = y_hi * 2 + y_lo), z: 16, core: 2. Of those that a mesh axis runs over, the one named last changes fastest.
Arguments:
- amplitudes: bfloat16 [32, 32, 512, 512], P('row', 'col', None, 'vir'), may hold values from -6 to 6
- integrals: bfloat16 [32, 32, 512, 512], P('row', 'col', 'vir'), may hold values from -0.15625 to 0.15625
- occ_irrep: int32 [32], replicated, may hold values from 0 to 7, as said below
- vir_irrep: int32 [512], replicated, may hold values from 0 to 7, as said below
Outputs:
- residual: float32 [32, 32, 512, 512], P('row', 'col', None, 'vir')
Inputs may be any that keep to these rules, and one draw needn't show every extreme that they name: `occ_irrep`: each of the 8 labels occurs among the occupied orbitals. `vir_irrep`: each of the 8 labels occurs among the virtual orbitals.
All inputs are finite; a program needn't handle non-finite values.
Results may differ from a plain program's by a relative error of at most 0.0052.
Values may be sent and summed in bfloat16 or wider, within the bound.
A program may use at most 64 MiB of HBM per device.

v0:
```python
import jax
import jax.numpy as jnp
from jax import lax
from jax.sharding import PartitionSpec as P


def from_partner(value, axis, apart):
    mask = 2**apart
    pairs = [(source, source ^ mask) for source in range(lax.axis_size(axis))]
    return lax.ppermute(value, axis, pairs)


def broadcast(value, axis, source):
    kept = jnp.where(lax.axis_index(axis) == source, value, 0).astype(value.dtype)
    return lax.psum(kept, axis)


def symmetry_mask(left, right, first, second):
    return (
        left[:, None, None, None]
        ^ right[None, :, None, None]
        ^ first[None, None, :, None]
        ^ second[None, None, None, :]
        == 0
    )


def contract(amplitude_tile, integral_tile):
    return jnp.einsum(
        "ikac,kjcb->ijab", amplitude_tile, integral_tile, preferred_element_type=jnp.float32
    )


def mirror(values, row_index, col_index):
    levels = lax.axis_size("row").bit_length() - 1
    for section_bit in range(levels):
        across = from_partner(values, "row", section_bit)
        across = from_partner(across, "col", section_bit)
        differ = row_index >> section_bit & 1 != col_index >> section_bit & 1
        values = jnp.where(differ, across, values)
    return values


def on_device(amplitudes, integrals, occ_irrep, vir_irrep):
    block_size = amplitudes.shape[0]
    virtual_count = amplitudes.shape[2]
    half_count = amplitudes.shape[3]
    row_index = lax.axis_index("row")
    col_index = lax.axis_index("col")
    half_index = lax.axis_index("vir")
    occ_row = lax.dynamic_slice_in_dim(occ_irrep, row_index * block_size, block_size)
    occ_col = lax.dynamic_slice_in_dim(occ_irrep, col_index * block_size, block_size)
    vir_half = lax.dynamic_slice_in_dim(vir_irrep, half_index * half_count, half_count)
    amp_masked = jnp.where(
        symmetry_mask(occ_row, occ_col, vir_irrep, vir_half), amplitudes, jnp.zeros_like(amplitudes)
    )
    int_masked = jnp.where(
        symmetry_mask(occ_row, occ_col, vir_half, vir_irrep), integrals, jnp.zeros_like(integrals)
    )
    flipped = lax.all_to_all(amp_masked, "vir", split_axis=2, concat_axis=3, tiled=True)
    combined = (
        2.0 * amp_masked.astype(jnp.float32)
        - jnp.transpose(flipped, (0, 1, 3, 2)).astype(jnp.float32)
    ).astype(jnp.bfloat16)
    off_diagonal = row_index != col_index
    empty_shape = (block_size, block_size, virtual_count, virtual_count)
    amp_row_diag = broadcast(combined, "col", row_index)
    int_col_diag = broadcast(int_masked, "row", col_index)
    own_term = contract(amp_row_diag, int_masked) + lax.cond(
        off_diagonal,
        lambda: contract(combined, int_col_diag),
        lambda: jnp.zeros(empty_shape, jnp.float32),
    )
    own_sum = lax.psum_scatter(
        own_term.astype(jnp.bfloat16), "vir", scatter_dimension=3, tiled=True
    )
    facing = mirror(own_sum, row_index, col_index)
    paired = lax.all_to_all(facing, "vir", split_axis=2, concat_axis=3, tiled=True)
    return own_sum.astype(jnp.float32) + jnp.transpose(paired, (1, 0, 3, 2)).astype(jnp.float32)


def solution(mesh):
    return jax.shard_map(
        on_device,
        mesh=mesh,
        in_specs=(P("row", "col", None, "vir"), P("row", "col", "vir", None), P(), P()),
        out_specs=P("row", "col", None, "vir"),
        check_vma=False,
    )
```

profile of v0, /device:TPU:25, one launch (start us, length us, event | category | flops | bytes accessed | tf_op | source)
XLA Modules:
  0.0 713.1 jit_solution(1141431673682749163)
XLA Ops:
  11.2 2.1 copy.12
  13.3 4.0 all-to-all-start
  17.3 11.9 %all-to-all-done = bf16[2,2,512,256]{3,1,0,2:T(2,128)(2,1)S(1)} async-done(((bf16[2,2,512,256]{3,1,0,2:T(2,128)(2,1)}), bf16[2,2,512,256]{3,1,0,2:T(2,128)(2,1)S(1)}, u32[]{:S(2)}, u32[]{:S(2)}) %all-to-all-start) | async-done | bytes 1048608 | tf_op jit(solution)/shard_map/all_to_all | solution.py:60
  30.1 2.6 copy.13
  32.8 2.8 broadcast_select_fusion.5
  35.7 133.3 %all-reduce.5.cloned.1.call-done = bf16[2,2,256,512]{2,3,0,1:T(8,128)(2,1)} async-done(((bf16[2,2,256,512]{2,3,0,1:T(8,128)(2,1)}), bf16[2,2,256,512]{2,3,0,1:T(8,128)(2,1)}) %all-reduce.5.cloned.1.call-update) | async-done | bytes 1048592 | tf_op jit(solution)/shard_map/psum | solution.py:15
  169.0 4.8 conditional.1
  169.0 4.8 convolution_bitcast_fusion
  173.8 129.8 %all-reduce.3.cloned.1.call-done = bf16[2,2,512,256]{3,2,1,0:T(8,128)(2,1)} async-done(((bf16[2,2,512,256]{3,2,1,0:T(8,128)(2,1)}), bf16[2,2,512,256]{3,2,1,0:T(8,128)(2,1)}) %all-reduce.3.cloned.1.call-update) | async-done | bytes 1048592 | tf_op jit(solution)/shard_map/psum | solution.py:15
  303.5 5.1 fusion.2
  308.7 47.7 %reduce-scatter.2.cloned.1.call-done = bf16[2,2,512,256]{2,3,0,1:T(8,128)(2,1)} async-done(((bf16[2,2,512,512]{2,3,0,1:T(8,128)(2,1)}), bf16[2,2,512,256]{2,3,0,1:T(8,128)(2,1)}) %reduce-scatter.2.cloned.1.call-update) | async-done | bytes 1048592 | tf_op jit(solution)/shard_map/reduce_scatter | solution.py:74
  356.3 2.6 collective-permute-start
  358.9 2.5 collective-permute-done
  361.4 3.2 collective-permute-start.1
  364.6 23.1 %collective-permute-done.1 = bf16[2,2,512,256]{2,3,0,1:T(8,128)(2,1)S(1)} collective-permute-done((bf16[2,2,512,256]{2,3,0,1:T(8,128)(2,1)S(1)}, bf16[2,2,512,256]{2,3,0,1:T(8,128)(2,1)S(1)}, u32[]{:S(2)}, u32[]{:S(2)}) %collective-permute-start.1) | collective-permute-done | bytes 1048608 | tf_op jit(solution)/shard_map/ppermute | solution.py:10
  387.8 3.1 collective-permute-start.2
  390.9 21.0 %collective-permute-done.2 = bf16[2,2,512,256]{2,3,0,1:T(8,128)(2,1)S(1)} collective-permute-done((bf16[2,2,512,256]{2,3,0,1:T(8,128)(2,1)S(1)}, bf16[2,2,512,256]{2,3,0,1:T(8,128)(2,1)S(1)}, u32[]{:S(2)}, u32[]{:S(2)}) %collective-permute-start.2) | collective-permute-done | bytes 1048608 | tf_op jit(solution)/shard_map/ppermute | solution.py:10
  411.9 4.2 collective-permute-start.3
  416.1 42.4 %collective-permute-done.3 = bf16[2,2,512,256]{2,3,0,1:T(8,128)(2,1)S(1)} collective-permute-done((bf16[2,2,512,256]{2,3,0,1:T(8,128)(2,1)S(1)}, bf16[2,2,512,256]{2,3,0,1:T(8,128)(2,1)S(1)}, u32[]{:S(2)}, u32[]{:S(2)}) %collective-permute-start.3) | collective-permute-done | bytes 1048608 | tf_op jit(solution)/shard_map/ppermute | solution.py:10
  458.6 4.6 collective-permute-start.4
  463.2 19.2 %collective-permute-done.4 = bf16[2,2,512,256]{2,3,0,1:T(8,128)(2,1)S(1)} collective-permute-done((bf16[2,2,512,256]{2,3,0,1:T(8,128)(2,1)S(1)}, bf16[2,2,512,256]{2,3,0,1:T(8,128)(2,1)S(1)}, u32[]{:S(2)}, u32[]{:S(2)}) %collective-permute-start.4) | collective-permute-done | bytes 1048608 | tf_op jit(solution)/shard_map/ppermute | solution.py:10
  482.3 7.3 %collective-permute-start.5 = (bf16[2,2,512,256]{2,3,0,1:T(8,128)(2,1)S(1)}, bf16[2,2,512,256]{2,3,0,1:T(8,128)(2,1)S(1)}, u32[]{:S(2)}, u32[]{:S(2)}) collective-permute-start(bf16[2,2,512,256]{2,3,0,1:T(8,128)(2,1)S(1)} %collective-permute-done.4), channel_id=1, source_target_pairs={{0,8},{2,10},{4,12},{6,14},{8,0},{10,2},{12,4},{14,6},{16,24},{18,... | collective-permute-start | bytes 3145736 | tf_op jit(solution)/shard_map/ppermute | solution.py:10
  489.7 90.0 %collective-permute-done.5 = bf16[2,2,512,256]{2,3,0,1:T(8,128)(2,1)S(1)} collective-permute-done((bf16[2,2,512,256]{2,3,0,1:T(8,128)(2,1)S(1)}, bf16[2,2,512,256]{2,3,0,1:T(8,128)(2,1)S(1)}, u32[]{:S(2)}, u32[]{:S(2)}) %collective-permute-start.5) | collective-permute-done | bytes 1048608 | tf_op jit(solution)/shard_map/ppermute | solution.py:10
  579.8 2.8 collective-permute-start.6
  582.6 24.9 %collective-permute-done.6 = bf16[2,2,512,256]{2,3,0,1:T(8,128)(2,1)S(1)} collective-permute-done((bf16[2,2,512,256]{2,3,0,1:T(8,128)(2,1)S(1)}, bf16[2,2,512,256]{2,3,0,1:T(8,128)(2,1)S(1)}, u32[]{:S(2)}, u32[]{:S(2)}) %collective-permute-start.6) | collective-permute-done | bytes 1048608 | tf_op jit(solution)/shard_map/ppermute | solution.py:10
  607.4 12.4 %collective-permute-start.7 = (bf16[2,2,512,256]{2,3,0,1:T(8,128)(2,1)S(1)}, bf16[2,2,512,256]{2,3,0,1:T(8,128)(2,1)S(1)}, u32[]{:S(2)}, u32[]{:S(2)}) collective-permute-start(bf16[2,2,512,256]{2,3,0,1:T(8,128)(2,1)S(1)} %collective-permute-done.6), channel_id=1, source_target_pairs={{0,16},{2,18},{4,20},{6,22},{8,24},{10,26},{12,28},{14,30},{16,0},... | collective-permute-start | bytes 3145736 | tf_op jit(solution)/shard_map/ppermute | solution.py:10
  619.9 60.4 %collective-permute-done.7 = bf16[2,2,512,256]{2,3,0,1:T(8,128)(2,1)S(1)} collective-permute-done((bf16[2,2,512,256]{2,3,0,1:T(8,128)(2,1)S(1)}, bf16[2,2,512,256]{2,3,0,1:T(8,128)(2,1)S(1)}, u32[]{:S(2)}, u32[]{:S(2)}) %collective-permute-start.7) | collective-permute-done | bytes 1048608 | tf_op jit(solution)/shard_map/ppermute | solution.py:10
  681.4 15.1 %all_to_all.8 = bf16[2,2,512,256]{3,0,1,2:T(2,128)(2,1)S(1)} all-to-all(bf16[2,2,512,256]{3,0,1,2:T(2,128)(2,1)S(1)} %copy.14), channel_id=1, replica_groups=mesh['row'=16,'col'=16,'vir'=2] {'vir'}, dimensions={2} | all-to-all | bytes 2097152 | tf_op jit(solution)/shard_map/all_to_all | solution.py:78
  696.5 2.4 copy.22
  698.9 3.0 reshape.57
  701.9 1.8 bitcast_add_fusion.1
  703.7 2.9 copy.16
  (28 shorter events, 7.1 us)
Async XLA Ops:
  6.5 2.5 copy-start.3
  6.5 162.4 %all-reduce.5.cloned.1.call-start = ((), (), s32[]{:S(2)}) async-start(), calls=%async_computation.4 | async-start | bytes 2097152 | tf_op jit(solution)/shard_map/psum | solution.py:15
  9.0 1.7 copy-start.2
  13.3 15.9 %all-to-all-start = ((bf16[2,2,512,256]{3,1,0,2:T(2,128)(2,1)}), bf16[2,2,512,256]{3,1,0,2:T(2,128)(2,1)S(1)}, u32[]{:S(2)}, u32[]{:S(2)}) async-start(bf16[2,2,512,256]{3,1,0,2:T(2,128)(2,1)} %copy.12), calls=%async_computation | async-start | bytes 2097152 | tf_op jit(solution)/shard_map/all_to_all | solution.py:60
  17.3 286.2 %all-reduce.3.cloned.1.call-start = ((), (), s32[]{:S(2)}) async-start(), calls=%async_computation.3 | async-start | bytes 2097152 | tf_op jit(solution)/shard_map/psum | solution.py:15
  29.2 1.0 copy-start.1
  35.6 320.7 %reduce-scatter.2.cloned.1.call-start = ((), (), s32[]{:S(2)}) async-start(), calls=%async_computation.5 | async-start | bytes 3145728 | tf_op jit(solution)/shard_map/reduce_scatter | solution.py:74
  356.3 5.1 collective-permute-start
  361.4 26.3 %collective-permute-start.1 = (bf16[2,2,512,256]{2,3,0,1:T(8,128)(2,1)S(1)}, bf16[2,2,512,256]{2,3,0,1:T(8,128)(2,1)S(1)}, u32[]{:S(2)}, u32[]{:S(2)}) collective-permute-start(bf16[2,2,512,256]{2,3,0,1:T(8,128)(2,1)S(1)} %collective-permute-done), channel_id=1, source_target_pairs={{0,2},{2,0},{4,6},{6,4},{8,10},{10,8},{12,14},{14,12},{16,18},{18,... | collective-permute-start | bytes 3145736 | tf_op jit(solution)/shard_map/ppermute | solution.py:10
  387.8 24.1 %collective-permute-start.2 = (bf16[2,2,512,256]{2,3,0,1:T(8,128)(2,1)S(1)}, bf16[2,2,512,256]{2,3,0,1:T(8,128)(2,1)S(1)}, u32[]{:S(2)}, u32[]{:S(2)}) collective-permute-start(bf16[2,2,512,256]{2,3,0,1:T(8,128)(2,1)S(1)} %broadcast_select_fusion), channel_id=1, source_target_pairs={{0,64},{32,96},{64,0},{96,32},{128,192},{160,224},{192,128},{224,1... | collective-permute-start | bytes 3145736 | tf_op jit(solution)/shard_map/ppermute | solution.py:10
  411.9 46.6 %collective-permute-start.3 = (bf16[2,2,512,256]{2,3,0,1:T(8,128)(2,1)S(1)}, bf16[2,2,512,256]{2,3,0,1:T(8,128)(2,1)S(1)}, u32[]{:S(2)}, u32[]{:S(2)}) collective-permute-start(bf16[2,2,512,256]{2,3,0,1:T(8,128)(2,1)S(1)} %collective-permute-done.2), channel_id=1, source_target_pairs={{0,4},{2,6},{4,0},{6,2},{8,12},{10,14},{12,8},{14,10},{16,20},{18,... | collective-permute-start | bytes 3145736 | tf_op jit(solution)/shard_map/ppermute | solution.py:10
  458.6 23.8 %collective-permute-start.4 = (bf16[2,2,512,256]{2,3,0,1:T(8,128)(2,1)S(1)}, bf16[2,2,512,256]{2,3,0,1:T(8,128)(2,1)S(1)}, u32[]{:S(2)}, u32[]{:S(2)}) collective-permute-start(bf16[2,2,512,256]{2,3,0,1:T(8,128)(2,1)S(1)} %broadcast_select_fusion.1), channel_id=1, source_target_pairs={{0,128},{32,160},{64,192},{96,224},{128,0},{160,32},{192,64},{224,... | collective-permute-start | bytes 3145736 | tf_op jit(solution)/shard_map/ppermute | solution.py:10
  482.3 97.3 %collective-permute-start.5 = (bf16[2,2,512,256]{2,3,0,1:T(8,128)(2,1)S(1)}, bf16[2,2,512,256]{2,3,0,1:T(8,128)(2,1)S(1)}, u32[]{:S(2)}, u32[]{:S(2)}) collective-permute-start(bf16[2,2,512,256]{2,3,0,1:T(8,128)(2,1)S(1)} %collective-permute-done.4), channel_id=1, source_target_pairs={{0,8},{2,10},{4,12},{6,14},{8,0},{10,2},{12,4},{14,6},{16,24},{18,... | collective-permute-start | bytes 3145736 | tf_op jit(solution)/shard_map/ppermute | solution.py:10
  579.8 27.6 %collective-permute-start.6 = (bf16[2,2,512,256]{2,3,0,1:T(8,128)(2,1)S(1)}, bf16[2,2,512,256]{2,3,0,1:T(8,128)(2,1)S(1)}, u32[]{:S(2)}, u32[]{:S(2)}) collective-permute-start(bf16[2,2,512,256]{2,3,0,1:T(8,128)(2,1)S(1)} %broadcast_select_fusion.2), channel_id=1, source_target_pairs={{0,256},{32,288},{64,320},{96,352},{128,384},{160,416},{192,448},{... | collective-permute-start | bytes 3145736 | tf_op jit(solution)/shard_map/ppermute | solution.py:10
  607.4 72.8 %collective-permute-start.7 = (bf16[2,2,512,256]{2,3,0,1:T(8,128)(2,1)S(1)}, bf16[2,2,512,256]{2,3,0,1:T(8,128)(2,1)S(1)}, u32[]{:S(2)}, u32[]{:S(2)}) collective-permute-start(bf16[2,2,512,256]{2,3,0,1:T(8,128)(2,1)S(1)} %collective-permute-done.6), channel_id=1, source_target_pairs={{0,16},{2,18},{4,20},{6,22},{8,24},{10,26},{12,28},{14,30},{16,0},... | collective-permute-start | bytes 3145736 | tf_op jit(solution)/shard_map/ppermute | solution.py:10
  698.9 3.0 copy-start
Sparse Core Ops, SparseCore 0:
  10.7 158.1 all-reduce.4
  171.4 132.0 all-reduce.2
  308.8 47.4 reduce-scatter.1
where the time goes:
time: 722 us; the launch traced here: 713 us
  waiting for transfers between devices  606 us (84%)
  starting transfers between devices  44.2 us (6%)
  local copies, waits for them, and re-layouts  17.4 us (2%)
  blocking collectives  15.1 us (2%)
  between operations  13.3 us (2%)
  matrix products  9.91 us (1%)
    ppermute x8, waiting for transfers between devices, from_partner(): return lax.ppermute(value, axis, pairs)  283 us
    psum x2, waiting for transfers between devices, broadcast(): return lax.psum(kept, axis)  263 us
    reduce_scatter x1, waiting for transfers between devices, on_device(): lax.psum_scatter(own_term.astype(jnp.bfloat16), 'vir', scatter_dimension=...  47.7 us
    ppermute x8, starting transfers between devices, from_partner(): return lax.ppermute(value, axis, pairs)  40.1 us
    all_to_all x1, blocking collectives, on_device(): lax.all_to_all(facing, 'vir', split_axis=2, concat_axis=3, tiled=True)  15.1 us
  transfers between devices with their start and end apart: 12, of which 12 were waited for; matrix products, arithmetic and copies ran while one was open for 2% of the time, Pallas kernels for 0%

commit v1 on v0

--- a/solution.py
+++ b/solution.py
@@ -1,7 +1,343 @@
+import functools
+
 import jax
 import jax.numpy as jnp
 from jax import lax
+from jax.experimental import pallas as pl
+from jax.experimental.pallas import tpu as pltpu
 from jax.sharding import PartitionSpec as P
+
+MESH = pl.DeviceIdType.MESH
+LABELS = 8
+SLOTS = 48
+F32 = jnp.float32
+BF16 = jnp.bfloat16
+
+COL_TREE = (
+    {0: 4, 4: 8, 8: 7, 12: 11, 11: 10, 5: 6, 3: 2, 15: 14},
+    {0: 12, 4: 5, 8: 9, 12: 13},
+    {0: 1, 4: 3},
+    {0: 15},
+)
+
+
+def lookup(key, table, default):
+    found = jnp.int32(default)
+    for at, value in table.items():
+        found = jnp.where(key == at, jnp.int32(value), found)
+    return found
+
+
+def dot(left, right, left_dim, right_dim):
+    return lax.dot_general(left, right, (((left_dim,), (right_dim,)), ((), ())), preferred_element_type=F32)
+
+
+def remote(src, dst, send_sem, recv_sem, device):
+    return pltpu.make_async_remote_copy(
+        src_ref=src, dst_ref=dst, send_sem=send_sem, recv_sem=recv_sem, device_id=device, device_id_type=MESH
+    )
+
+
+def column_of(row_labels):
+    return jnp.broadcast_to(row_labels, (128, row_labels.shape[1])).T[:, :1]
+
+
+def slot_matrix(labels, slots):
+    count = labels.shape[1]
+    is_label = (lax.broadcasted_iota(jnp.int32, (LABELS, count), 0) == labels).astype(F32)
+    earlier = (
+        lax.broadcasted_iota(jnp.int32, (count, count), 0) < lax.broadcasted_iota(jnp.int32, (count, count), 1)
+    ).astype(F32)
+    before = dot(is_label.astype(BF16), earlier.astype(BF16), 1, 0)
+    rank = jnp.sum(before * is_label, axis=0, keepdims=True)
+    slot = lax.broadcasted_iota(jnp.int32, (slots, count), 0).astype(F32)
+    return jnp.where(slot == rank, 1.0, 0.0).astype(BF16)
+
+
+def cycle_kernel(
+    amp, itg, vir, occ, own, mirrored, slot_out,
+    amp_own, int_own, amp_diag, int_diag, v_send, v_recv, part, part_recv, mid,
+    v_ss, v_rs, col_ss, col_rs, row_ss, row_rs, part_ss, part_rs, hop_ss, hop_rs, end_ss, end_rs,
+):
+    slots = SLOTS
+    half = amp.shape[3]
+    I, J, h = lax.axis_index("row"), lax.axis_index("col"), lax.axis_index("vir")
+    other = 1 - h
+    diagonal = I == J
+    partner = (I, J, other)
+
+    apart = lax.rem(J - I + 16, 16)
+    col_child = [lookup(apart, table, -1) for table in COL_TREE]
+    col_parent = lookup(apart, {b: a for table in COL_TREE for a, b in table.items()}, 0)
+
+    def along_col(offset):
+        return (I, lax.rem(I + offset + 16, 16), h)
+
+    dy = lax.rem(I // 8 + J // 8, 2)
+    dx = lax.rem(lax.rem(I // 2, 4) - lax.rem(J // 2, 4) + 4, 4)
+    dc = lax.rem(I + J, 2)
+
+    def at_plane(y, x, core):
+        row = lax.rem(J // 8 + y, 2) * 8 + lax.rem(lax.rem(J // 2, 4) + x, 4) * 2 + lax.rem(J + core, 2)
+        return (row, J, h)
+
+    first = dc == 0
+    row_child = [
+        (first, at_plane(dy, dx, 1)),
+        (jnp.logical_and(first, dx == 0), at_plane(dy, 3, 0)),
+        (jnp.logical_and(first, dx <= 1), at_plane(dy, dx + 1, 0)),
+        (jnp.logical_and(first, dx + dy == 0), at_plane(1, 0, 0)),
+    ]
+    parent_y = jnp.where(jnp.logical_and(first, dx == 0), 0, dy)
+    parent_x = jnp.where(first, jnp.where(dx == 2, 1, 0), dx)
+    row_parent = at_plane(parent_y, parent_x, 0)
+
+    r, s = I // 2, J // 2
+    mid_row = lax.rem(5 * r + s, 8) * 2 + lax.rem(I, 2)
+    from_row = lax.rem(5 * (r - s + 8), 8) * 2 + lax.rem(I, 2)
+    back_row = lax.rem(5 * s + r, 8) * 2 + lax.rem(J, 2)
+    mid_self = mid_row == I
+    from_self = from_row == I
+    end_self = jnp.logical_and(from_row == J, I == J)
+    end_at = (J, from_row, h)
+
+    barrier = pltpu.get_barrier_semaphore()
+
+    def greet(device):
+        pl.semaphore_signal(barrier, inc=1, device_id=device, device_id_type=MESH)
+
+    greet(partner)
+
+    @pl.when(jnp.logical_not(diagonal))
+    def _():
+        greet(along_col(col_parent))
+        greet(row_parent)
+
+    for v in range(2):
+        @pl.when(jnp.logical_not(jnp.logical_and(from_self, h == v)))
+        def _():
+            greet((from_row, J, v))
+
+    back_self = jnp.logical_and(back_row == I, I == J)
+
+    @pl.when(jnp.logical_not(back_self))
+    def _():
+        greet((back_row, I, h))
+
+    labels = [vir[:, w * half:(w + 1) * half] for w in range(2)]
+    labels_here = jnp.where(h == 0, labels[0], labels[1])
+    slot_of = [slot_matrix(labels[w], slots) for w in range(2)]
+    for w in range(2):
+        slot_out[:, w * half:(w + 1) * half] = slot_of[w]
+    slot_here = jnp.where(h == 0, slot_of[0].astype(F32), slot_of[1].astype(F32)).astype(BF16)
+    column = column_of(vir[...])
+    column_here = jnp.where(h == 0, column[:half], column[half:])
+    all_row = vir[...]
+
+    cross_amp = column ^ labels_here
+    cross_int = column_here ^ all_row
+    for i in range(2):
+        for k in range(2):
+            g = occ[2 * I + i] ^ occ[2 * J + k]
+            kept = jnp.where(cross_amp == g, amp[i, k].astype(F32), 0.0).astype(BF16)
+            packed = dot(slot_here, kept, 1, 1)
+            flipped = [dot(slot_of[w], kept[w * half:(w + 1) * half], 1, 0) for w in range(2)]
+            flipped_here = jnp.where(h == 0, flipped[0], flipped[1])
+            v_send[i * 2 + k] = jnp.where(h == 0, flipped[1], flipped[0]).astype(BF16)
+            for w in range(2):
+                piece = 2.0 * packed[:, w * half:(w + 1) * half]
+                amp_own[i * 2 + k, :, w * half:(w + 1) * half] = jnp.where(h == w, piece - flipped_here, piece).astype(BF16)
+            kept_int = jnp.where(cross_int == g, itg[i, k].astype(F32), 0.0).astype(BF16)
+            int_own[k * 2 + i] = dot(slot_here, kept_int, 1, 0).astype(BF16)
+
+    expected = jnp.int32(1)
+    for child in col_child:
+        expected += jnp.where(child >= 0, 1, 0)
+    for there, _ in row_child:
+        expected += jnp.where(there, 1, 0)
+    expected += jnp.where(mid_self, 1, 2)
+    expected += jnp.where(end_self, 0, 1)
+    pl.semaphore_wait(barrier, expected)
+
+    def v_copy(q):
+        return remote(v_send.at[q], v_recv.at[q], v_ss.at[q], v_rs.at[q], partner)
+
+    def col_copy(q, n):
+        return remote(amp_diag.at[q], amp_diag.at[q], col_ss.at[n, q], col_rs.at[q], along_col(col_child[n]))
+
+    def row_copy(q, n):
+        return remote(int_diag.at[q], int_diag.at[q], row_ss.at[n, q], row_rs.at[q], row_child[n][1])
+
+    def part_copy(q):
+        return remote(part.at[other, q], part_recv.at[q], part_ss.at[q], part_rs.at[q], partner)
+
+    def hop_copy(q, v, slot):
+        return remote(own.at[v, q], mid.at[slot, q], hop_ss.at[v, q], hop_rs.at[slot, q], (mid_row, J, v))
+
+    def end_copy(q, v):
+        return remote(mid.at[v, q], mirrored.at[v, q], end_ss.at[v, q], end_rs.at[v, q], end_at)
+
+    for q in range(4):
+        v_copy(q).start()
+
+    @pl.when(diagonal)
+    def _():
+        int_diag[...] = int_own[...]
+
+    def row_forward(q):
+        for n, (there, _) in reversed(list(enumerate(row_child))):
+            @pl.when(there)
+            def _():
+                row_copy(q, n).start()
+
+    def col_forward(q):
+        for n, child in enumerate(col_child):
+            @pl.when(child >= 0)
+            def _():
+                col_copy(q, n).start()
+
+    @pl.when(diagonal)
+    def _():
+        for q in range(4):
+            row_forward(q)
+
+    rest = pl.ds(pl.multiple_of(other * half, half), half)
+    for q in range(4):
+        v_copy(q).wait_recv()
+        amp_own[q, :, rest] = (amp_own[q, :, rest].astype(F32) - v_recv[q].astype(F32)).astype(BF16)
+
+        @pl.when(diagonal)
+        def _():
+            amp_diag[q] = amp_own[q]
+            amp_own[q] = jnp.zeros(amp_own.shape[1:], BF16)
+            col_forward(q)
+
+    @pl.when(jnp.logical_not(diagonal))
+    def _():
+        for q in range(4):
+            row_copy(q, 0).wait_recv()
+            row_forward(q)
+        for q in range(4):
+            col_copy(q, 0).wait_recv()
+            col_forward(q)
+
+    def both(ref, n):
+        return ref[2 * n:2 * n + 2].reshape(2 * slots, 2 * half)
+
+    cross = column ^ all_row
+    for i in range(2):
+        for j in range(2):
+            g = occ[2 * I + i] ^ occ[2 * J + j]
+            total = dot(both(int_own, j), both(amp_diag, i), 0, 0) + dot(both(int_diag, j), both(amp_own, i), 0, 0)
+            total = jnp.where(cross == g, total, 0.0).astype(BF16)
+            q = i * 2 + j
+            for w in range(2):
+                part[w, q] = dot(slot_of[w], total[w * half:(w + 1) * half], 1, 0).astype(BF16)
+            part_copy(q).start()
+
+    for q in range(4):
+        part_copy(q).wait_recv()
+        cycle = (part[h, q].astype(F32) + part_recv[q].astype(F32)).astype(BF16)
+        for v in range(2):
+            own[v, q] = cycle[:, v * half:(v + 1) * half]
+            to_self = jnp.logical_and(mid_self, h == v)
+
+            @pl.when(to_self)
+            def _():
+                mid[v, q] = own[v, q]
+
+            @pl.when(jnp.logical_not(to_self))
+            def _():
+                hop_copy(q, v, h).start()
+
+    for q in range(4):
+        for v in range(2):
+            @pl.when(jnp.logical_not(jnp.logical_and(from_self, h == v)))
+            def _():
+                hop_copy(q, v, v).wait_recv()
+
+            @pl.when(end_self)
+            def _():
+                mirrored[v, q] = mid[v, q]
+
+            @pl.when(jnp.logical_not(end_self))
+            def _():
+                end_copy(q, v).start()
+
+    for q in range(4):
+        for v in range(2):
+            @pl.when(jnp.logical_not(back_self))
+            def _():
+                end_copy(q, v).wait_recv()
+
+    for q in range(4):
+        v_copy(q).wait_send()
+        part_copy(q).wait_send()
+        for n, child in enumerate(col_child):
+            @pl.when(child >= 0)
+            def _():
+                col_copy(q, n).wait_send()
+        for n, (there, _) in enumerate(row_child):
+            @pl.when(there)
+            def _():
+                row_copy(q, n).wait_send()
+        for v in range(2):
+            @pl.when(jnp.logical_not(jnp.logical_and(mid_self, h == v)))
+            def _():
+                hop_copy(q, v, v).wait_send()
+
+            @pl.when(jnp.logical_not(end_self))
+            def _():
+                end_copy(q, v).wait_send()
+
+
+def unpack_kernel(own, mirrored, slot_of, vir, occ, out):
+    half = out.shape[3]
+    I, J, h = lax.axis_index("row"), lax.axis_index("col"), lax.axis_index("vir")
+    i, j = pl.program_id(0), pl.program_id(1)
+    g = occ[2 * I + i] ^ occ[2 * J + j]
+    here = pl.ds(pl.multiple_of(h * half, half), half)
+    cross = column_of(vir[...]) ^ vir[:, here]
+    for v in range(2):
+        rows = slice(v * half, (v + 1) * half)
+        left = jnp.concatenate([own[v, i * 2 + j], slot_of[:, rows]], axis=0)
+        right = jnp.concatenate([slot_of[:, here], mirrored[v, j * 2 + i]], axis=0)
+        out[0, 0, rows] = jnp.where(cross[rows] == g, dot(left, right, 0, 0), 0.0)
+
+
+def packed_plan(amplitudes, integrals, occ_irrep, vir_irrep):
+    half = amplitudes.shape[3]
+    full = 2 * half
+    vmem = pl.BlockSpec(memory_space=pltpu.VMEM)
+    smem = pl.BlockSpec(memory_space=pltpu.SMEM)
+    vir = vir_irrep.reshape(1, full)
+    tile = pltpu.VMEM((4, SLOTS, full), BF16)
+    dma = pltpu.SemaphoreType.DMA
+    halves = jax.ShapeDtypeStruct((2, 4, SLOTS, half), BF16)
+    own, mirrored, slot_of = pl.pallas_call(
+        cycle_kernel,
+        out_shape=[halves, halves, jax.ShapeDtypeStruct((SLOTS, full), BF16)],
+        in_specs=[vmem, vmem, vmem, smem],
+        out_specs=[vmem, vmem, vmem],
+        scratch_shapes=[
+            tile, tile, tile, tile,
+            pltpu.VMEM((4, SLOTS, half), BF16), pltpu.VMEM((4, SLOTS, half), BF16),
+            pltpu.VMEM((2, 4, SLOTS, full), BF16), tile, pltpu.VMEM((2, 4, SLOTS, half), BF16),
+            dma((4,)), dma((4,)), dma((4, 4)), dma((4,)), dma((4, 4)), dma((4,)), dma((4,)), dma((4,)),
+            dma((2, 4)), dma((2, 4)), dma((2, 4)), dma((2, 4)),
+        ],
+        compiler_params=pltpu.CompilerParams(
+            collective_id=0, has_side_effects=True, vmem_limit_bytes=32 * 2**20
+        ),
+    )(amplitudes, integrals, vir, occ_irrep)
+    return pl.pallas_call(
+        unpack_kernel,
+        grid=(2, 2),
+        out_shape=jax.ShapeDtypeStruct((2, 2, full, half), F32),
+        in_specs=[vmem, vmem, vmem, vmem, smem],
+        out_specs=pl.BlockSpec((1, 1, full, half), lambda i, j: (i, j, 0, 0)),
+        compiler_params=pltpu.CompilerParams(vmem_limit_bytes=32 * 2**20),
+    )(own, mirrored, slot_of, vir, occ_irrep)
 
 
 def from_partner(value, axis, apart):
@@ -41,7 +377,7 @@
     return values
 
 
-def on_device(amplitudes, integrals, occ_irrep, vir_irrep):
+def whole_plan(amplitudes, integrals, occ_irrep, vir_irrep):
     block_size = amplitudes.shape[0]
     virtual_count = amplitudes.shape[2]
     half_count = amplitudes.shape[3]
@@ -79,6 +415,12 @@
     return own_sum.astype(jnp.float32) + jnp.transpose(paired, (1, 0, 3, 2)).astype(jnp.float32)
 
 
+def on_device(amplitudes, integrals, occ_irrep, vir_irrep):
+    halves = vir_irrep.reshape(2, -1, 1) == jnp.arange(LABELS, dtype=jnp.int32)
+    most = jnp.max(jnp.sum(halves.astype(jnp.int32), axis=1))
+    return lax.cond(most <= SLOTS, packed_plan, whole_plan, amplitudes, integrals, occ_irrep, vir_irrep)
+
+
 def solution(mesh):
     return jax.shard_map(
         on_device,

time: 722 us -> 80.1 us (0.11); the launches traced: 713 us -> 80 us
  waiting for transfers between devices: 606 us -> 0 us
  Pallas kernels: 0 us -> 63 us
  starting transfers between devices: 44.2 us -> 0 us
  local copies, waits for them, and re-layouts: 17.4 us -> 2.02 us
  blocking collectives: 15.1 us -> 0 us
  matrix products: 9.91 us -> 0 us
    ppermute x8 -> x0, waiting for transfers between devices: 283 us -> none  [from_partner(): return lax.ppermute(value, axis, pairs)]
    psum x2 -> x0, waiting for transfers between devices: 263 us -> none  [broadcast(): return lax.psum(kept, axis)]
    pallas_call x0 -> x2, Pallas kernels: none -> 63 us  [the longest x1 61 us: packed_plan(): pl.pallas_call(cycle_kernel, out_shape=[halves, halves, jax.ShapeDtypeStr...]
    reduce_scatter x1 -> x0, waiting for transfers between devices: 47.7 us -> none  [on_device(): lax.psum_scatter(own_term.astype(jnp.bfloat16), 'vir', scatter_dimension=...]
    ppermute x8 -> x0, starting transfers between devices: 40.1 us -> none  [from_partner(): return lax.ppermute(value, axis, pairs)]
    all_to_all x1 -> x0, blocking collectives: 15.1 us -> none  [on_device(): lax.all_to_all(facing, 'vir', split_axis=2, concat_axis=3, tiled=True)]
    all_to_all x1 -> x0, waiting for transfers between devices: 11.9 us -> none  [on_device(): lax.all_to_all(amp_masked, 'vir', split_axis=2, concat_axis=3, tiled=True)]
    dot_general x2 -> x0, matrix products: 9.91 us -> none  [contract(): jnp.einsum('ikac,kjcb->ijab', amplitude_tile, integral_tile, preferred_el...]
  transfers between devices with their start and end apart: 12 -> 0, of which waited for: 12 -> 0; matrix products, arithmetic and copies ran while one was open for 2% -> 0% of each run, Pallas kernels for 0% -> 0%
where the time goes in v1:
time: 80.1 us; the launch traced here: 80 us
  Pallas kernels  63 us (79%)
  between operations  14 us (17%)
  local copies, waits for them, and re-layouts  2.02 us (3%)
    pallas_call x1, Pallas kernels, packed_plan(): pl.pallas_call(cycle_kernel, out_shape=[halves, halves, jax.ShapeDtypeStr...  61 us
    pallas_call x1, Pallas kernels, packed_plan(): pl.pallas_call(unpack_kernel, grid=(2, 2), out_shape=jax.ShapeDtypeStruct...  2.02 us

profile of v1, /device:TPU:25, one launch (start us, length us, event | category | flops | bytes accessed | tf_op | source)
XLA Modules:
  0.0 80.0 jit_solution(2869218045153064333)
XLA Ops:
  6.5 0.7 eq.27
  7.2 0.1 convert_reduce_fusion
  7.4 0.6 reduce_max.9
  8.7 63.1 %conditional.2 = (f32[2,2,512,256]{3,2,1,0:T(8,128)S(1)}) conditional(s32[]{:T(128)} %convert_element_type.56, (s32[32]{0:T(128)}, s32[512]{0:T(512)}, bf16[2,2,256,512]{3,2,1,0:T(8,128)(2,1)}, bf16[2,2,512,256]{3,2,1,0:T(8,128)(2,1)}) %tuple.17, (s32[512]{0:T(512)}, bf16[2,2,512,256]{3,2,1,0:T(8,128)(2,1)}, bf16[2,2,256,512]{3,2,1,0:T(8,128)(2,1)}, ...), branch_computations={%region_2.8_spmd, %region_8.9_spmd} | conditional | flops 2163215360 | bytes 132178144 | solution.py:421
  8.7 0.0 copy-start.4
  8.7 0.0 copy-start.5
  8.7 61.0 %branch_1_fun.2 = (bf16[2,4,48,256]{3,2,1,0:T(8,128)(2,1)S(1)}, bf16[2,4,48,256]{3,2,1,0:T(8,128)(2,1)S(1)}, bf16[48,512]{1,0:T(8,128)(2,1)S(1)}) custom-call(bf16[2,2,512,256]{3,2,1,0:T(8,128)(2,1)} %get-tuple-element.37.amp, bf16[2,2,256,512]{3,2,1,0:T(8,128)(2,1)} %get-tuple-element.38.itg, s32[1,512]{1,0:T(1,128)} %bitcast.50, s32[32]{0:T(128)} %get-tuple-element.40.occ), custom_call_target="tpu_custom_call" | custom-call | tf_op jit(solution)/shard_map/cond/branch_1_fun/pallas_call | solution.py:317
  69.7 0.0 copy-done.4
  69.8 0.0 copy-done.5
  69.8 2.0 %branch_1_fun.3 = f32[2,2,512,256]{3,2,1,0:T(8,128)S(1)} custom-call(bf16[2,4,48,256]{3,2,1,0:T(8,128)(2,1)S(1)} %get-tuple-element.41.own, bf16[2,4,48,256]{3,2,1,0:T(8,128)(2,1)S(1)} %get-tuple-element.42.mirrored, bf16[48,512]{1,0:T(8,128)(2,1)S(1)} %get-tuple-element.43.slot_of, s32[1,512]{1,0:T(1,128)S(1)} %bitcast.51, s32[32]{0:T(128)S(1)} %copy-done.5), custom_call_target="tpu_custom_call" | custom-call | tf_op jit(solution)/shard_map/cond/branch_1_fun/pallas_call | solution.py:333
  71.8 0.0 copy-start.2
  71.8 1.3 %copy-done.2 = f32[2,2,512,256]{3,2,1,0:T(8,128)} copy-done((f32[2,2,512,256]{3,2,1,0:T(8,128)}, f32[2,2,512,256]{3,2,1,0:T(8,128)S(1)}, u32[]{:S(2)}) %copy-start.2) | copy-done | bytes 2097176
Async XLA Ops:
  8.7 61.1 %copy-start.4 = (s32[512]{0:T(512)S(1)}, s32[512]{0:T(512)}, u32[]{:S(2)}) copy-start(s32[512]{0:T(512)} %get-tuple-element.39) | copy-start | bytes 6148 | tf_op jit(solution)/shard_map/cond
  8.7 61.1 %copy-start.5 = (s32[32]{0:T(128)S(1)}, s32[32]{0:T(128)}, u32[]{:S(2)}) copy-start(s32[32]{0:T(128)} %get-tuple-element.40.occ) | copy-start | bytes 388 | tf_op jit(solution)/shard_map/cond
  71.8 1.3 %copy-start.2 = (f32[2,2,512,256]{3,2,1,0:T(8,128)}, f32[2,2,512,256]{3,2,1,0:T(8,128)S(1)}, u32[]{:S(2)}) copy-start(f32[2,2,512,256]{3,2,1,0:T(8,128)S(1)} %get-tuple-element.85) | copy-start | bytes 6291460

commit v2 on v1

--- a/solution.py
+++ b/solution.py
@@ -55,14 +55,17 @@
 
 
 def cycle_kernel(
-    amp, itg, vir, occ, own, mirrored, slot_out,
-    amp_own, int_own, amp_diag, int_diag, v_send, v_recv, part, part_recv, mid,
+    amp_hbm, int_hbm, vir, occ, own, mirrored, slot_out,
+    amp, itg, load_sem, amp_own, int_own, amp_diag, int_diag, v_send, v_recv, part, part_recv, mid,
     v_ss, v_rs, col_ss, col_rs, row_ss, row_rs, part_ss, part_rs, hop_ss, hop_rs, end_ss, end_rs,
 ):
     slots = SLOTS
     half = amp.shape[3]
     I, J, h = lax.axis_index("row"), lax.axis_index("col"), lax.axis_index("vir")
     other = 1 - h
+    loads = [pltpu.make_async_copy(amp_hbm, amp, load_sem.at[0]), pltpu.make_async_copy(int_hbm, itg, load_sem.at[1])]
+    for load in loads:
+        load.start()
     diagonal = I == J
     partner = (I, J, other)
 
@@ -134,6 +137,8 @@
     column_here = jnp.where(h == 0, column[:half], column[half:])
     all_row = vir[...]
 
+    for load in loads:
+        load.wait()
     cross_amp = column ^ labels_here
     cross_int = column_here ^ all_row
     for i in range(2):
@@ -317,9 +322,10 @@
     own, mirrored, slot_of = pl.pallas_call(
         cycle_kernel,
         out_shape=[halves, halves, jax.ShapeDtypeStruct((SLOTS, full), BF16)],
-        in_specs=[vmem, vmem, vmem, smem],
+        in_specs=[pl.BlockSpec(memory_space=pl.ANY)] * 2 + [vmem, smem],
         out_specs=[vmem, vmem, vmem],
         scratch_shapes=[
+            pltpu.VMEM(amplitudes.shape, BF16), pltpu.VMEM(integrals.shape, BF16), dma((2,)),
             tile, tile, tile, tile,
             pltpu.VMEM((4, SLOTS, half), BF16), pltpu.VMEM((4, SLOTS, half), BF16),
             pltpu.VMEM((2, 4, SLOTS, full), BF16), tile, pltpu.VMEM((2, 4, SLOTS, half), BF16),
@@ -340,15 +346,27 @@
     )(own, mirrored, slot_of, vir, occ_irrep)
 
 
-def from_partner(value, axis, apart):
-    mask = 2**apart
-    pairs = [(source, source ^ mask) for source in range(lax.axis_size(axis))]
-    return lax.ppermute(value, axis, pairs)
-
-
-def broadcast(value, axis, source):
-    kept = jnp.where(lax.axis_index(axis) == source, value, 0).astype(value.dtype)
-    return lax.psum(kept, axis)
+def from_diagonal(value, row_index, col_index, along):
+    size = lax.axis_size("col")
+    apart = (col_index - row_index if along == "col" else row_index - col_index) % size
+    reach = 1
+    while reach < size:
+        pairs = []
+        for near in range(size):
+            for step in range(reach):
+                source, target = (near + step) % size, (near + step + reach) % size
+                if along == "col":
+                    pairs.append((near * size + source, near * size + target))
+                else:
+                    pairs.append((source * size + near, target * size + near))
+        moved = lax.ppermute(value, ("row", "col"), pairs)
+        value = jnp.where(jnp.logical_and(apart >= reach, apart < 2 * reach), moved, value)
+        reach *= 2
+    return value
+
+
+def from_other_half(value):
+    return lax.ppermute(value, "vir", [(0, 1), (1, 0)])
 
 
 def symmetry_mask(left, right, first, second):
@@ -367,14 +385,10 @@
     )
 
 
-def mirror(values, row_index, col_index):
-    levels = lax.axis_size("row").bit_length() - 1
-    for section_bit in range(levels):
-        across = from_partner(values, "row", section_bit)
-        across = from_partner(across, "col", section_bit)
-        differ = row_index >> section_bit & 1 != col_index >> section_bit & 1
-        values = jnp.where(differ, across, values)
-    return values
+def from_mirror(value):
+    size = lax.axis_size("col")
+    pairs = [(i * size + j, j * size + i) for i in range(size) for j in range(size)]
+    return lax.ppermute(value, ("row", "col"), pairs)
 
 
 def whole_plan(amplitudes, integrals, occ_irrep, vir_irrep):
@@ -400,17 +414,18 @@
     ).astype(jnp.bfloat16)
     off_diagonal = row_index != col_index
     empty_shape = (block_size, block_size, virtual_count, virtual_count)
-    amp_row_diag = broadcast(combined, "col", row_index)
-    int_col_diag = broadcast(int_masked, "row", col_index)
+    amp_row_diag = from_diagonal(combined, row_index, col_index, "col")
+    int_col_diag = from_diagonal(int_masked, row_index, col_index, "row")
     own_term = contract(amp_row_diag, int_masked) + lax.cond(
         off_diagonal,
         lambda: contract(combined, int_col_diag),
         lambda: jnp.zeros(empty_shape, jnp.float32),
     )
-    own_sum = lax.psum_scatter(
-        own_term.astype(jnp.bfloat16), "vir", scatter_dimension=3, tiled=True
-    )
-    facing = mirror(own_sum, row_index, col_index)
+    rounded = own_term.astype(jnp.bfloat16)
+    kept = lax.dynamic_slice_in_dim(rounded, half_index * half_count, half_count, 3)
+    moved = from_other_half(lax.dynamic_slice_in_dim(rounded, (1 - half_index) * half_count, half_count, 3))
+    own_sum = (kept.astype(jnp.float32) + moved.astype(jnp.float32)).astype(jnp.bfloat16)
+    facing = from_mirror(own_sum)
     paired = lax.all_to_all(facing, "vir", split_axis=2, concat_axis=3, tiled=True)
     return own_sum.astype(jnp.float32) + jnp.transpose(paired, (1, 0, 3, 2)).astype(jnp.float32)
 

time: 80.1 us -> 66.3 us (0.83)
  between operations: 14 us -> 0.67 us
where the time goes in v2:
time: 66.3 us; the launch traced here: 66.1 us
  Pallas kernels  62.3 us (94%)
  local copies, waits for them, and re-layouts  2.02 us (3%)
  other arithmetic  0.79 us (1%)
  between operations  0.67 us (1%)
    pallas_call x1, Pallas kernels, packed_plan(): pl.pallas_call(cycle_kernel, out_shape=[halves, halves, jax.ShapeDtypeStr...  60.3 us
    pallas_call x1, Pallas kernels, packed_plan(): pl.pallas_call(unpack_kernel, grid=(2, 2), out_shape=jax.ShapeDtypeStruct...  2.02 us

profile of v2, /device:TPU:25, one launch (start us, length us, event | category | flops | bytes accessed | tf_op | source)
XLA Modules:
  0.0 66.1 jit_solution(3379842916201899476)
XLA Ops:
  0.0 0.7 %eq.24 = s32[2,256]{1,0:T(2,128)S(1)} reshape(s32[512]{0:T(512)} %param.11) | data formatting | bytes 4096 | tf_op jit(solution)/shard_map/eq | solution.py:434
  0.7 0.1 convert_reduce_fusion
  0.8 0.6 reduce_max.9
  2.1 62.6 %conditional.2 = (f32[2,2,512,256]{3,2,1,0:T(8,128)S(1)}) conditional(s32[]{:T(128)} %convert_element_type.61, (s32[32]{0:T(128)}, s32[512]{0:T(512)}, bf16[2,2,256,512]{3,2,1,0:T(8,128)(2,1)}, bf16[2,2,512,256]{3,2,1,0:T(8,128)(2,1)}) %tuple.17, (s32[512]{0:T(512)}, bf16[2,2,512,256]{3,2,1,0:T(8,128)(2,1)}, bf16[2,2,256,512]{3,2,1,0:T(8,128)(2,1)}, ...), branch_computations={%region_2.5_spmd, %region_5.6_spmd} | conditional | flops 2165312512 | bytes 156328352 | solution.py:436
  2.4 0.0 copy-start.6
  2.4 0.0 copy-start.7
  2.4 60.3 %branch_1_fun.2 = (bf16[2,4,48,256]{3,2,1,0:T(8,128)(2,1)S(1)}, bf16[2,4,48,256]{3,2,1,0:T(8,128)(2,1)S(1)}, bf16[48,512]{1,0:T(8,128)(2,1)S(1)}) custom-call(bf16[2,2,512,256]{3,2,1,0:T(8,128)(2,1)} %get-tuple-element.51.amp_hbm, bf16[2,2,256,512]{3,2,1,0:T(8,128)(2,1)} %get-tuple-element.52.int_hbm, s32[1,512]{1,0:T(1,128)} %bitcast.49, ...), custom_call_target="tpu_custom_call" | custom-call | tf_op jit(solution)/shard_map/cond/branch_1_fun/pallas_call | solution.py:322
  62.7 0.0 copy-done.6
  62.7 0.0 copy-done.7
  62.7 2.0 %branch_1_fun.3 = f32[2,2,512,256]{3,2,1,0:T(8,128)S(1)} custom-call(bf16[2,4,48,256]{3,2,1,0:T(8,128)(2,1)S(1)} %get-tuple-element.55.own, bf16[2,4,48,256]{3,2,1,0:T(8,128)(2,1)S(1)} %get-tuple-element.56.mirrored, bf16[48,512]{1,0:T(8,128)(2,1)S(1)} %get-tuple-element.57.slot_of, s32[1,512]{1,0:T(1,128)S(1)} %bitcast.50, s32[32]{0:T(128)S(1)} %copy-done.7), custom_call_target="tpu_custom_call" | custom-call | tf_op jit(solution)/shard_map/cond/branch_1_fun/pallas_call | solution.py:339
  64.8 0.0 copy-start.4
  64.8 1.3 %copy-done.4 = f32[2,2,512,256]{3,2,1,0:T(8,128)} copy-done((f32[2,2,512,256]{3,2,1,0:T(8,128)}, f32[2,2,512,256]{3,2,1,0:T(8,128)S(1)}, u32[]{:S(2)}) %copy-start.4) | copy-done | bytes 2097176
Async XLA Ops:
  2.4 60.4 %copy-start.6 = (s32[512]{0:T(512)S(1)}, s32[512]{0:T(512)}, u32[]{:S(2)}) copy-start(s32[512]{0:T(512)} %get-tuple-element.53) | copy-start | bytes 6148 | tf_op jit(solution)/shard_map/cond
  2.4 60.3 %copy-start.7 = (s32[32]{0:T(128)S(1)}, s32[32]{0:T(128)}, u32[]{:S(2)}) copy-start(s32[32]{0:T(128)} %get-tuple-element.54.occ) | copy-start | bytes 388 | tf_op jit(solution)/shard_map/cond
  64.8 1.3 %copy-start.4 = (f32[2,2,512,256]{3,2,1,0:T(8,128)}, f32[2,2,512,256]{3,2,1,0:T(8,128)S(1)}, u32[]{:S(2)}) copy-start(f32[2,2,512,256]{3,2,1,0:T(8,128)S(1)} %get-tuple-element.95) | copy-start | bytes 6291460

commit v3 on v2

--- a/solution.py
+++ b/solution.py
@@ -14,9 +14,10 @@
 BF16 = jnp.bfloat16
 
 COL_TREE = (
-    {0: 4, 4: 8, 8: 7, 12: 11, 11: 10, 5: 6, 3: 2, 15: 14},
-    {0: 12, 4: 5, 8: 9, 12: 13},
-    {0: 1, 4: 3},
+    {0: 8, 8: 7, 4: 5, 5: 6, 12: 11, 11: 10, 1: 2, 15: 14},
+    {0: 4, 8: 9, 4: 3, 12: 13},
+    {0: 12},
+    {0: 1},
     {0: 15},
 )
 
@@ -51,11 +52,11 @@
     before = dot(is_label.astype(BF16), earlier.astype(BF16), 1, 0)
     rank = jnp.sum(before * is_label, axis=0, keepdims=True)
     slot = lax.broadcasted_iota(jnp.int32, (slots, count), 0).astype(F32)
-    return jnp.where(slot == rank, 1.0, 0.0).astype(BF16)
+    return jnp.where(slot == rank, 1.0, 0.0).astype(BF16), jnp.max(rank)
 
 
 def cycle_kernel(
-    amp_hbm, int_hbm, vir, occ, own, mirrored, slot_out,
+    amp_hbm, int_hbm, vir, occ, own, mirrored, slot_out, most_out,
     amp, itg, load_sem, amp_own, int_own, amp_diag, int_diag, v_send, v_recv, part, part_recv, mid,
     v_ss, v_rs, col_ss, col_rs, row_ss, row_rs, part_ss, part_rs, hop_ss, hop_rs, end_ss, end_rs,
 ):
@@ -87,12 +88,13 @@
     first = dc == 0
     row_child = [
         (first, at_plane(dy, dx, 1)),
+        (jnp.logical_and(first, dx == 0), at_plane(dy, 2, 0)),
         (jnp.logical_and(first, dx == 0), at_plane(dy, 3, 0)),
-        (jnp.logical_and(first, dx <= 1), at_plane(dy, dx + 1, 0)),
+        (jnp.logical_and(first, dx == 0), at_plane(dy, 1, 0)),
         (jnp.logical_and(first, dx + dy == 0), at_plane(1, 0, 0)),
     ]
     parent_y = jnp.where(jnp.logical_and(first, dx == 0), 0, dy)
-    parent_x = jnp.where(first, jnp.where(dx == 2, 1, 0), dx)
+    parent_x = jnp.where(first, 0, dx)
     row_parent = at_plane(parent_y, parent_x, 0)
 
     r, s = I // 2, J // 2
@@ -129,7 +131,9 @@
 
     labels = [vir[:, w * half:(w + 1) * half] for w in range(2)]
     labels_here = jnp.where(h == 0, labels[0], labels[1])
-    slot_of = [slot_matrix(labels[w], slots) for w in range(2)]
+    (slot_low, most_low), (slot_high, most_high) = [slot_matrix(labels[w], slots) for w in range(2)]
+    slot_of = [slot_low, slot_high]
+    most_out[...] = jnp.full((1, 1), jnp.maximum(most_low, most_high), F32)
     for w in range(2):
         slot_out[:, w * half:(w + 1) * half] = slot_of[w]
     slot_here = jnp.where(h == 0, slot_of[0].astype(F32), slot_of[1].astype(F32)).astype(BF16)
@@ -217,14 +221,22 @@
             amp_own[q] = jnp.zeros(amp_own.shape[1:], BF16)
             col_forward(q)
 
-    @pl.when(jnp.logical_not(diagonal))
+    @pl.when(jnp.logical_and(first, jnp.logical_not(diagonal)))
     def _():
         for q in range(4):
             row_copy(q, 0).wait_recv()
             row_forward(q)
+
+    @pl.when(jnp.logical_not(diagonal))
+    def _():
         for q in range(4):
             col_copy(q, 0).wait_recv()
             col_forward(q)
+
+    @pl.when(jnp.logical_not(first))
+    def _():
+        for q in range(4):
+            row_copy(q, 0).wait_recv()
 
     def both(ref, n):
         return ref[2 * n:2 * n + 2].reshape(2 * slots, 2 * half)
@@ -245,18 +257,19 @@
         cycle = (part[h, q].astype(F32) + part_recv[q].astype(F32)).astype(BF16)
         for v in range(2):
             own[v, q] = cycle[:, v * half:(v + 1) * half]
-            to_self = jnp.logical_and(mid_self, h == v)
-
-            @pl.when(to_self)
-            def _():
-                mid[v, q] = own[v, q]
-
-            @pl.when(jnp.logical_not(to_self))
-            def _():
-                hop_copy(q, v, h).start()
-
-    for q in range(4):
-        for v in range(2):
+
+        @pl.when(mid_self)
+        def _():
+            mid[h, q] = own[h, q]
+
+        @pl.when(jnp.logical_not(mid_self))
+        def _():
+            hop_copy(q, h, h).start()
+
+        hop_copy(q, other, h).start()
+
+    for q in range(4):
+        for v in (h, other):
             @pl.when(jnp.logical_not(jnp.logical_and(from_self, h == v)))
             def _():
                 hop_copy(q, v, v).wait_recv()
@@ -310,7 +323,7 @@
         out[0, 0, rows] = jnp.where(cross[rows] == g, dot(left, right, 0, 0), 0.0)
 
 
-def packed_plan(amplitudes, integrals, occ_irrep, vir_irrep):
+def packed_cycle(amplitudes, integrals, occ_irrep, vir_irrep):
     half = amplitudes.shape[3]
     full = 2 * half
     vmem = pl.BlockSpec(memory_space=pltpu.VMEM)
@@ -319,23 +332,30 @@
     tile = pltpu.VMEM((4, SLOTS, full), BF16)
     dma = pltpu.SemaphoreType.DMA
     halves = jax.ShapeDtypeStruct((2, 4, SLOTS, half), BF16)
-    own, mirrored, slot_of = pl.pallas_call(
+    return pl.pallas_call(
         cycle_kernel,
-        out_shape=[halves, halves, jax.ShapeDtypeStruct((SLOTS, full), BF16)],
+        out_shape=[halves, halves, jax.ShapeDtypeStruct((SLOTS, full), BF16), jax.ShapeDtypeStruct((1, 1), F32)],
         in_specs=[pl.BlockSpec(memory_space=pl.ANY)] * 2 + [vmem, smem],
-        out_specs=[vmem, vmem, vmem],
+        out_specs=[vmem, vmem, vmem, vmem],
         scratch_shapes=[
             pltpu.VMEM(amplitudes.shape, BF16), pltpu.VMEM(integrals.shape, BF16), dma((2,)),
             tile, tile, tile, tile,
             pltpu.VMEM((4, SLOTS, half), BF16), pltpu.VMEM((4, SLOTS, half), BF16),
             pltpu.VMEM((2, 4, SLOTS, full), BF16), tile, pltpu.VMEM((2, 4, SLOTS, half), BF16),
-            dma((4,)), dma((4,)), dma((4, 4)), dma((4,)), dma((4, 4)), dma((4,)), dma((4,)), dma((4,)),
+            dma((4,)), dma((4,)), dma((5, 4)), dma((4,)), dma((5, 4)), dma((4,)), dma((4,)), dma((4,)),
             dma((2, 4)), dma((2, 4)), dma((2, 4)), dma((2, 4)),
         ],
         compiler_params=pltpu.CompilerParams(
             collective_id=0, has_side_effects=True, vmem_limit_bytes=32 * 2**20
         ),
     )(amplitudes, integrals, vir, occ_irrep)
+
+
+def packed_sum(own, mirrored, slot_of, occ_irrep, vir_irrep):
+    half = own.shape[3]
+    full = 2 * half
+    vmem = pl.BlockSpec(memory_space=pltpu.VMEM)
+    smem = pl.BlockSpec(memory_space=pltpu.SMEM)
     return pl.pallas_call(
         unpack_kernel,
         grid=(2, 2),
@@ -343,7 +363,7 @@
         in_specs=[vmem, vmem, vmem, vmem, smem],
         out_specs=pl.BlockSpec((1, 1, full, half), lambda i, j: (i, j, 0, 0)),
         compiler_params=pltpu.CompilerParams(vmem_limit_bytes=32 * 2**20),
-    )(own, mirrored, slot_of, vir, occ_irrep)
+    )(own, mirrored, slot_of, vir_irrep.reshape(1, full), occ_irrep)
 
 
 def from_diagonal(value, row_index, col_index, along):
@@ -431,9 +451,12 @@
 
 
 def on_device(amplitudes, integrals, occ_irrep, vir_irrep):
-    halves = vir_irrep.reshape(2, -1, 1) == jnp.arange(LABELS, dtype=jnp.int32)
-    most = jnp.max(jnp.sum(halves.astype(jnp.int32), axis=1))
-    return lax.cond(most <= SLOTS, packed_plan, whole_plan, amplitudes, integrals, occ_irrep, vir_irrep)
+    own, mirrored, slot_of, last_rank = packed_cycle(amplitudes, integrals, occ_irrep, vir_irrep)
+    return lax.cond(
+        last_rank[0, 0] < SLOTS,
+        lambda: packed_sum(own, mirrored, slot_of, occ_irrep, vir_irrep),
+        lambda: whole_plan(amplitudes, integrals, occ_irrep, vir_irrep),
+    )
 
 
 def solution(mesh):

time: 66.3 us -> 62.3 us (0.940)
  Pallas kernels: 62.3 us -> 59.2 us
  other arithmetic: 0.79 us -> 0 us
  local copies, waits for them, and re-layouts: 2.02 us -> 1.32 us
    pallas_call x2, Pallas kernels: 62.3 us -> 59.2 us  [the longest x1 56.9 us: packed_cycle(): pl.pallas_call(cycle_kernel, out_shape=[halves, halves, jax.ShapeDtypeStr...]
    eq x1 -> x0, local copies, waits for them, and re-layouts: 0.69 us -> none  [on_device(): halves = vir_irrep.reshape(2, -1, 1) == jnp.arange(LABELS, dtype=jnp.int32)]
where the time goes in v3:
time: 62.3 us; the launch traced here: 61.5 us
  Pallas kernels  59.2 us (95%)
  local copies, waits for them, and re-layouts  1.32 us (2%)
  between operations  0.74 us (1%)
    pallas_call x1, Pallas kernels, packed_cycle(): pl.pallas_call(cycle_kernel, out_shape=[halves, halves, jax.ShapeDtypeStr...  56.9 us
    pallas_call x1, Pallas kernels, packed_sum(): pl.pallas_call(unpack_kernel, grid=(2, 2), out_shape=jax.ShapeDtypeStruct...  2.3 us
    unnamed x8, local copies, waits for them, and re-layouts  1.32 us

profile of v3, /device:TPU:25, one launch (start us, length us, event | category | flops | bytes accessed | tf_op | source)
XLA Modules:
  0.0 61.5 jit_solution(9276735738836453930)
XLA Ops:
  0.0 0.0 copy-start.1
  0.0 0.0 copy-start.5
  0.0 0.0 copy-start.6
  0.0 56.9 %shard_map.48 = (bf16[2,4,48,256]{3,2,1,0:T(8,128)(2,1)S(1)}, bf16[2,4,48,256]{3,2,1,0:T(8,128)(2,1)S(1)}, bf16[48,512]{1,0:T(8,128)(2,1)}, f32[1,1]{1,0:T(1,128)}) custom-call(bf16[2,2,512,256]{3,2,1,0:T(8,128)(2,1)} %amp_hbm.1, bf16[2,2,256,512]{3,2,1,0:T(8,128)(2,1)} %int_hbm.1, s32[1,512]{1,0:T(1,128)} %bitcast.51, s32[32]{0:T(128)} %occ.1), custom_call_target="tpu_custom_call" | custom-call | tf_op jit(solution)/shard_map/pallas_call | solution.py:335
  57.6 0.0 copy-done.1
  57.6 0.0 copy-done.5
  57.6 0.0 copy-done.6
  57.6 2.5 %conditional.2 = (f32[2,2,512,256]{3,2,1,0:T(8,128)S(1)}) conditional(s32[]{:T(128)} %bitcast.21, (s32[32]{0:T(128)S(1)}, s32[512]{0:T(512)S(1)}, bf16[2,2,256,512]{3,2,1,0:T(8,128)(2,1)}, bf16[2,2,512,256]{3,2,1,0:T(8,128)(2,1)S(1)}) %tuple.37, (s32[512]{0:T(512)S(1)}, bf16[2,4,48,256]{3,2,1,0:T(8,128)(2,1)S(1)}, ...), branch_computations={%region_0.3_spmd, %region_3.4_spmd} | conditional | flops 2165312512 | bytes 152125792 | solution.py:455
  57.8 2.3 %branch_1_fun.1 = f32[2,2,512,256]{3,2,1,0:T(8,128)S(1)} custom-call(bf16[2,4,48,256]{3,2,1,0:T(8,128)(2,1)S(1)} %get-tuple-element.53.own, bf16[2,4,48,256]{3,2,1,0:T(8,128)(2,1)S(1)} %get-tuple-element.54.mirrored, bf16[48,512]{1,0:T(8,128)(2,1)} %get-tuple-element.55.slot_of, s32[1,512]{1,0:T(1,128)S(1)} %bitcast.52, s32[32]{0:T(128)S(1)} %get-tuple-element.57.occ), custom_call_target="tpu_custom_call" | custom-call | tf_op jit(solution)/shard_map/cond/branch_1_fun/pallas_call | solution.py:359
  60.1 0.0 copy-start.4
  60.2 1.3 %copy-done.4 = f32[2,2,512,256]{3,2,1,0:T(8,128)} copy-done((f32[2,2,512,256]{3,2,1,0:T(8,128)}, f32[2,2,512,256]{3,2,1,0:T(8,128)S(1)}, u32[]{:S(2)}) %copy-start.4) | copy-done | bytes 2097176
Async XLA Ops:
  0.0 57.6 %copy-start.1 = (bf16[2,2,512,256]{3,2,1,0:T(8,128)(2,1)S(1)}, bf16[2,2,512,256]{3,2,1,0:T(8,128)(2,1)}, u32[]{:S(2)}) copy-start(bf16[2,2,512,256]{3,2,1,0:T(8,128)(2,1)} %amp_hbm.1) | copy-start | bytes 3145732
  0.0 57.6 %copy-start.5 = (s32[512]{0:T(512)S(1)}, s32[512]{0:T(512)}, u32[]{:S(2)}) copy-start(s32[512]{0:T(512)} %param.11) | copy-start | bytes 6148
  0.0 57.6 %copy-start.6 = (s32[32]{0:T(128)S(1)}, s32[32]{0:T(128)}, u32[]{:S(2)}) copy-start(s32[32]{0:T(128)} %occ.1) | copy-start | bytes 388
  60.1 1.3 %copy-start.4 = (f32[2,2,512,256]{3,2,1,0:T(8,128)}, f32[2,2,512,256]{3,2,1,0:T(8,128)S(1)}, u32[]{:S(2)}) copy-start(f32[2,2,512,256]{3,2,1,0:T(8,128)S(1)} %get-tuple-element.94) | copy-start | bytes 6291460

commit v4 on v3

--- a/solution.py
+++ b/solution.py
@@ -14,9 +14,9 @@
 BF16 = jnp.bfloat16
 
 COL_TREE = (
-    {0: 8, 8: 7, 4: 5, 5: 6, 12: 11, 11: 10, 1: 2, 15: 14},
-    {0: 4, 8: 9, 4: 3, 12: 13},
-    {0: 12},
+    {0: 8, 8: 7, 4: 6, 12: 10, 1: 2, 15: 14},
+    {0: 4, 8: 9, 4: 5, 12: 11},
+    {0: 12, 4: 3, 12: 13},
     {0: 1},
     {0: 15},
 )

time: 62.3 us -> 61.9 us (level)
  the two profiles are of different devices: /device:TPU:25 before, /device:TPU:17 now
where the time goes in v4:
time: 61.9 us; the launch traced here: 61.7 us
  Pallas kernels  59.3 us (96%)
  local copies, waits for them, and re-layouts  1.32 us (2%)
  between operations  0.74 us (1%)
    pallas_call x1, Pallas kernels, packed_cycle(): pl.pallas_call(cycle_kernel, out_shape=[halves, halves, jax.ShapeDtypeStr...  57 us
    pallas_call x1, Pallas kernels, packed_sum(): pl.pallas_call(unpack_kernel, grid=(2, 2), out_shape=jax.ShapeDtypeStruct...  2.31 us
    unnamed x8, local copies, waits for them, and re-layouts  1.32 us

profile of v4, /device:TPU:17, one launch (start us, length us, event | category | flops | bytes accessed | tf_op | source)
XLA Modules:
  0.0 61.7 jit_solution(9345463325493751010)
XLA Ops:
  0.0 0.0 copy-start.1
  0.0 0.0 copy-start.5
  0.0 0.0 copy-start.6
  0.0 57.0 %shard_map.48 = (bf16[2,4,48,256]{3,2,1,0:T(8,128)(2,1)S(1)}, bf16[2,4,48,256]{3,2,1,0:T(8,128)(2,1)S(1)}, bf16[48,512]{1,0:T(8,128)(2,1)}, f32[1,1]{1,0:T(1,128)}) custom-call(bf16[2,2,512,256]{3,2,1,0:T(8,128)(2,1)} %amp_hbm.1, bf16[2,2,256,512]{3,2,1,0:T(8,128)(2,1)} %int_hbm.1, s32[1,512]{1,0:T(1,128)} %bitcast.51, s32[32]{0:T(128)} %occ.1), custom_call_target="tpu_custom_call" | custom-call | tf_op jit(solution)/shard_map/pallas_call | solution.py:335
  57.8 0.0 copy-done.1
  57.8 0.0 copy-done.5
  57.8 0.0 copy-done.6
  57.8 2.5 %conditional.2 = (f32[2,2,512,256]{3,2,1,0:T(8,128)S(1)}) conditional(s32[]{:T(128)} %bitcast.21, (s32[32]{0:T(128)S(1)}, s32[512]{0:T(512)S(1)}, bf16[2,2,256,512]{3,2,1,0:T(8,128)(2,1)}, bf16[2,2,512,256]{3,2,1,0:T(8,128)(2,1)S(1)}) %tuple.37, (s32[512]{0:T(512)S(1)}, bf16[2,4,48,256]{3,2,1,0:T(8,128)(2,1)S(1)}, ...), branch_computations={%region_0.3_spmd, %region_3.4_spmd} | conditional | flops 2165312512 | bytes 152125792 | solution.py:455
  58.0 2.3 %branch_1_fun.1 = f32[2,2,512,256]{3,2,1,0:T(8,128)S(1)} custom-call(bf16[2,4,48,256]{3,2,1,0:T(8,128)(2,1)S(1)} %get-tuple-element.53.own, bf16[2,4,48,256]{3,2,1,0:T(8,128)(2,1)S(1)} %get-tuple-element.54.mirrored, bf16[48,512]{1,0:T(8,128)(2,1)} %get-tuple-element.55.slot_of, s32[1,512]{1,0:T(1,128)S(1)} %bitcast.52, s32[32]{0:T(128)S(1)} %get-tuple-element.57.occ), custom_call_target="tpu_custom_call" | custom-call | tf_op jit(solution)/shard_map/cond/branch_1_fun/pallas_call | solution.py:359
  60.3 0.0 copy-start.4
  60.3 1.3 %copy-done.4 = f32[2,2,512,256]{3,2,1,0:T(8,128)} copy-done((f32[2,2,512,256]{3,2,1,0:T(8,128)}, f32[2,2,512,256]{3,2,1,0:T(8,128)S(1)}, u32[]{:S(2)}) %copy-start.4) | copy-done | bytes 2097176
Async XLA Ops:
  0.0 57.8 %copy-start.1 = (bf16[2,2,512,256]{3,2,1,0:T(8,128)(2,1)S(1)}, bf16[2,2,512,256]{3,2,1,0:T(8,128)(2,1)}, u32[]{:S(2)}) copy-start(bf16[2,2,512,256]{3,2,1,0:T(8,128)(2,1)} %amp_hbm.1) | copy-start | bytes 3145732
  0.0 57.8 %copy-start.5 = (s32[512]{0:T(512)S(1)}, s32[512]{0:T(512)}, u32[]{:S(2)}) copy-start(s32[512]{0:T(512)} %param.11) | copy-start | bytes 6148
  0.0 57.8 %copy-start.6 = (s32[32]{0:T(128)S(1)}, s32[32]{0:T(128)}, u32[]{:S(2)}) copy-start(s32[32]{0:T(128)} %occ.1) | copy-start | bytes 388
  60.3 1.3 %copy-start.4 = (f32[2,2,512,256]{3,2,1,0:T(8,128)}, f32[2,2,512,256]{3,2,1,0:T(8,128)S(1)}, u32[]{:S(2)}) copy-start(f32[2,2,512,256]{3,2,1,0:T(8,128)S(1)} %get-tuple-element.94) | copy-start | bytes 6291460
